TPU v7x, 32 devices: a whole 2x2x4 slice. The times are simulated.
32 devices in a mesh: groups: 1, ffn: 32 (over z, y, x, core), mp: 1.
Axes of the slice: x: 2, y: 2, z: 4, core: 2. Of those that a mesh axis runs over, the one named last changes fastest.
Arguments:
- hidden_in: bfloat16 [128, 4096], P(('groups', 'ffn'), 'mp'), may hold values from -6 to 6
- out_grad: bfloat16 [128, 4096], P(('groups', 'ffn'), 'mp'), may hold values from -0.796875 to 0.796875
- step_ids: int32 [128], P(('groups', 'ffn')), may hold values from 0 to 7
- segment_ids: int32 [128], P(('groups', 'ffn')), may hold values from 0 to 3, never falling along the last dimension, each value on 1 to 64 neighbouring positions
- advantage_codes: int32 [128], P(('groups', 'ffn')), may hold values from -8 to 8
- gate_weight: bfloat16 [4096, 7168], P('mp', 'ffn'), may hold values from -0.09375 to 0.09375
- up_weight: bfloat16 [4096, 7168], P('mp', 'ffn'), may hold values from -0.09375 to 0.09375
- down_weight: bfloat16 [7168, 4096], P('ffn', 'mp'), may hold values from -0.0625 to 0.0625
Outputs:
- input_grad: bfloat16 [128, 4096], P(('groups', 'ffn'), 'mp')
- gate_grad: bfloat16 [4096, 7168], P(('groups', 'mp'), 'ffn')
- up_grad: bfloat16 [4096, 7168], P(('groups', 'mp'), 'ffn')
- down_grad: bfloat16 [7168, 4096], P(('groups', 'ffn'), 'mp')
All inputs are finite; a program needn't handle non-finite values.
Results may differ from a plain program's by a relative error of at most 0.0057.
Values may be sent and summed in bfloat16 or wider, within the bound.
A program may use at most 64 MiB of HBM per device.

v0:
```python
import math

import jax
import jax.numpy as jnp
from jax import lax
from jax.sharding import PartitionSpec as P


def advantage_weights(steps, segments, codes):
    same = segments[:, None] == segments[None, :]
    later = steps[None, :] >= steps[:, None]
    gap = (steps[None, :] - steps[:, None]).astype(jnp.float32)
    kernel = jnp.where(same & later, jnp.exp(gap * math.log(0.75)), jnp.zeros_like(gap))
    total = jnp.dot(kernel, codes.astype(jnp.float32), precision=lax.Precision.HIGHEST)
    count = jnp.sum(same.astype(jnp.float32), axis=1)
    return total / (8.0 * jnp.sqrt(count))


def contract_last(left, right):
    return lax.dot_general(
        left, right, (((1,), (1,)), ((), ())), preferred_element_type=jnp.float32
    )


def contract_first(left, right):
    return lax.dot_general(
        left, right, (((0,), (0,)), ((), ())), preferred_element_type=jnp.float32
    )


def local(
    hidden_in, out_grad, step_ids, segment_ids, advantage_codes, gate_weight, up_weight, down_weight
):
    inputs_all, grads_all = (
        lax.all_gather(hidden_in, "ffn", axis=0, tiled=True),
        lax.all_gather(out_grad, "ffn", axis=0, tiled=True),
    )
    labels = lax.all_gather(
        jnp.stack([step_ids, segment_ids, advantage_codes]), "ffn", axis=1, tiled=True
    )
    advantage = advantage_weights(labels[0], labels[1], labels[2])
    weighted = (advantage[:, None] * grads_all.astype(jnp.float32)).astype(jnp.bfloat16)
    gate_part = jnp.dot(inputs_all, gate_weight, preferred_element_type=jnp.float32)
    up_part = jnp.dot(inputs_all, up_weight, preferred_element_type=jnp.float32)
    gate_pre, up_pre = lax.psum((gate_part, up_part), "mp")
    sigma = jax.nn.sigmoid(gate_pre)
    hidden = (gate_pre * sigma * up_pre).astype(jnp.bfloat16)
    hidden_grad = lax.psum(contract_last(weighted, down_weight), "mp")
    up_delta = (hidden_grad * gate_pre * sigma).astype(jnp.bfloat16)
    gate_delta = (hidden_grad * up_pre * sigma * (1.0 + gate_pre * (1.0 - sigma))).astype(
        jnp.bfloat16
    )
    down_grad = contract_first(hidden, weighted).astype(jnp.bfloat16)
    gate_grad = contract_first(inputs_all, gate_delta).astype(jnp.bfloat16)
    up_grad = contract_first(inputs_all, up_delta).astype(jnp.bfloat16)
    partial_grad = contract_last(gate_delta, gate_weight) + contract_last(up_delta, up_weight)
    input_grad = lax.psum_scatter(partial_grad, "ffn", scatter_dimension=0, tiled=True)
    return (input_grad.astype(jnp.bfloat16), gate_grad, up_grad, down_grad)


def solution(mesh):
    in_specs = (
        P(("groups", "ffn"), "mp"),
        P(("groups", "ffn"), "mp"),
        P(("groups", "ffn")),
        P(("groups", "ffn")),
        P(("groups", "ffn")),
        P("mp", "ffn"),
        P("mp", "ffn"),
        P("ffn", "mp"),
    )
    out_specs = (
        P(("groups", "ffn"), "mp"),
        P(("groups", "mp"), "ffn"),
        P(("groups", "mp"), "ffn"),
        P(("groups", "ffn"), "mp"),
    )
    return jax.shard_map(local, mesh=mesh, in_specs=in_specs, out_specs=out_specs, check_vma=False)
```

profile of v0, /device:TPU:0, one launch (start us, length us, event | category | flops | bytes accessed | tf_op | source)
XLA Modules:
  0.0 203.9 jit_solution(17771594333427321504)
XLA Ops:
  7.2 0.0 copy-start
  7.2 0.0 all-gather.8.cloned.1.call-start
  7.2 0.7 all-gather.8.cloned.1.call-update
  7.9 0.0 all-gather.6.cloned.1.call-start
  8.0 0.7 all-gather.6.cloned.1.call-update
  8.7 0.7 add_bitcast_fusion
  9.4 0.1 copy.16
  9.5 43.4 %all-gather = s32[32,4,3]{2,1,0:T(4,128)S(1)} all-gather(s32[1,4,3]{2,1,0:T(4,128)S(1)} %bitcast.42), channel_id=1, replica_groups=mesh['groups'=1,'ffn'=32,'mp'=1] {'ffn'}, dimensions={0}, use_global_device_ids=true | all-gather | bytes 1584 | tf_op jit(solution)/shard_map/all_gather | solution.py:38
  52.8 0.1 copy.17
  52.9 0.2 fusion.3
  53.1 0.3 fusion.2
  53.4 13.9 %all-gather.8.cloned.1.call-done = bf16[32,4,4096]{2,1,0:T(4,128)(2,1)} async-done(((bf16[1,4,4096]{2,1,0:T(4,128)(2,1)}), bf16[32,4,4096]{2,1,0:T(4,128)(2,1)}) %all-gather.8.cloned.1.call-update) | async-done | bytes 1048592 | tf_op jit(solution)/shard_map/all_gather | solution.py:35
  67.3 1.3 reshape.17
  68.6 2.1 %fusion.24 = f32[128,224]{0,1:T(8,128)S(1)} fusion(bf16[128,4096]{1,0:T(8,128)(2,1)S(1)} %reshape.17, bf16[4096,224]{0,1:T(8,128)(2,1)} %param.14), kind=kOutput, calls=%fused_computation.40 | convolution fusion | flops 234881024 | bytes 2998272 | tf_op jit(solution)/shard_map/dot_general | solution.py:44
  70.8 0.0 copy-done
  70.8 0.6 fusion.25
  71.4 51.4 %all-gather.6.cloned.1.call-done = bf16[32,4,4096]{2,1,0:T(4,128)(2,1)} async-done(((bf16[1,4,4096]{2,1,0:T(4,128)(2,1)}), bf16[32,4,4096]{2,1,0:T(4,128)(2,1)}) %all-gather.6.cloned.1.call-update) | async-done | bytes 1048592 | tf_op jit(solution)/shard_map/all_gather | solution.py:36
  122.8 2.5 %reshape.18 = f32[128,4096]{1,0:T(8,128)} reshape(bf16[32,4,4096]{2,1,0:T(4,128)(2,1)} %all-gather.6.cloned.1.call-done) | data formatting | bytes 3145728 | tf_op jit(solution)/shard_map/convert_element_type | solution.py:42
  125.3 2.8 %multiply_convert_fusion.2 = (bf16[128,224]{0,1:T(8,128)(2,1)S(1)}, bf16[128,224]{0,1:T(8,128)(2,1)S(1)}) fusion(f32[128,224]{0,1:T(8,128)S(1)} %fusion.25, f32[128,224]{0,1:T(8,128)S(1)} %fusion.24, bf16[224,4096]{1,0:T(8,128)(2,1)} %param.15, f32[128,4096]{1,0:T(8,128)} %reshape.18, f32[128]{0:T(128)S(1)} %fusion.2), kind=kOutput, calls=%fused_computation.10 | convolution fusion | flops 236302336 | bytes 4276736 | tf_op jit(solution)/shard_map/dot_general | solution.py:20
  128.1 0.5 fusion.26
  128.6 0.0 copy-start.1
  128.6 1.9 fusion
  130.5 0.0 copy-done.1
  130.5 1.9 convolution_convert_fusion
  132.4 0.0 copy-start.2
  132.4 1.9 fusion.1
  134.3 0.0 copy-done.2
  134.3 1.8 convolution_add_fusion
  136.1 60.3 %all-reduce.2 = bf16[128,4096]{1,0:T(8,128)(2,1)S(1)} all-reduce(f32[128,4096]{1,0:T(8,128)} %convolution_add_fusion), channel_id=2, replica_groups=mesh['groups'=1,'ffn'=32,'mp'=1] {'ffn'}, use_global_device_ids=true, to_apply=%region_1.2.clone | all-reduce | flops 524288 | bytes 3145728
  196.4 0.6 dynamic-slice_convert_fusion
  (1 shorter events, 0.0 us)
Async XLA Ops:
  7.2 63.6 %copy-start = (bf16[4096,224]{0,1:T(8,128)(2,1)S(1)}, bf16[4096,224]{0,1:T(8,128)(2,1)}, u32[]{:S(2)}) copy-start(bf16[4096,224]{0,1:T(8,128)(2,1)} %param.13) | copy-start | bytes 5505028
  7.2 60.1 %all-gather.8.cloned.1.call-start = ((), (), s32[]{:S(2)}) async-start(), calls=%async_computation.1 | async-start | bytes 1081344 | tf_op jit(solution)/shard_map/all_gather | solution.py:35
  7.9 114.9 %all-gather.6.cloned.1.call-start = ((), (), s32[]{:S(2)}) async-start(), calls=%async_computation | async-start | bytes 1081344 | tf_op jit(solution)/shard_map/all_gather | solution.py:36
  128.6 1.9 copy-start.1
  132.4 1.9 copy-start.2
Sparse Core Ops, SparseCore 0:
  10.9 56.3 all-gather.7
  70.1 52.6 all-gather.5
where the time goes:
time: 204 us
  blocking collectives  104 us (51%)
  waiting for transfers between devices  66.7 us (33%)
  between operations  14.1 us (7%)
  matrix products  13.8 us (7%)
  local copies, waits for them, and re-layouts  4.61 us (2%)
    unnamed x1, blocking collectives  60.3 us
    all_gather x1, waiting for transfers between devices, local(): lax.all_gather(out_grad, 'ffn', axis=0, tiled=True)  51.4 us
    all_gather x1, blocking collectives, local(): lax.all_gather(jnp.stack([step_ids, segment_ids, advantage_codes]), 'ffn'...  43.4 us
    all_gather x1, waiting for transfers between devices, local(): lax.all_gather(hidden_in, 'ffn', axis=0, tiled=True)  13.9 us
    dot_general x3, matrix products, contract_first(): lax.dot_general(left, right, (((0,), (0,)), ((), ())), preferred_element_...  5.64 us
    dot_general x3, matrix products, contract_last(): lax.dot_general(left, right, (((1,), (1,)), ((), ())), preferred_element_...  5.14 us
  transfers between devices with their start and end apart: 2, of which 2 were waited for; matrix products, arithmetic and copies ran while one was open for 3% of the time, Pallas kernels for 0%

commit v1 on v0

--- a/solution.py
+++ b/solution.py
@@ -3,6 +3,8 @@
 import jax
 import jax.numpy as jnp
 from jax import lax
+from jax.experimental import pallas as pl
+from jax.experimental.pallas import tpu as pltpu
 from jax.sharding import PartitionSpec as P
 
 
@@ -26,6 +28,331 @@
     return lax.dot_general(
         left, right, (((0,), (0,)), ((), ())), preferred_element_type=jnp.float32
     )
+
+
+BF = jnp.bfloat16
+F32 = jnp.float32
+MESH = pl.DeviceIdType.MESH
+LANES = 128
+
+
+def gather_kernel(
+    x_ref, g_ref, step_ref, segment_ref, code_ref, gate_hbm, up_hbm, down_hbm,
+    input_grad_ref, x_out, weighted_out, hidden_out, gate_delta_out, up_delta_out,
+    gate_w, up_w, down_w, raw, rows, part, core_out, core_in, sums, first_out, first_in,
+    halves, second_out, second_in, blocks, last_keep, last_out, last_in,
+    weight_sem, up_send, up_recv, dn_send, dn_recv, l_send, l_recv,
+    core_send, core_recv, first_send, first_recv, second_send, second_recv, z_send, z_recv,
+):
+    features = x_ref.shape[1]
+    wide = features // 4
+    me = lax.axis_index("ffn")
+    z = me // 8
+    y = lax.rem(me // 4, 2)
+    x = lax.rem(me // 2, 2)
+    core = lax.rem(me, 2)
+    mate = me + 1 - 2 * core
+    xnbr = me + 2 - 4 * x
+    ynbr = me + 4 - 8 * y
+
+    loads = [
+        pltpu.make_async_copy(src, dst, weight_sem.at[i])
+        for i, (src, dst) in enumerate(((gate_hbm, gate_w), (up_hbm, up_w), (down_hbm, down_w)))
+    ]
+    for load in loads:
+        load.start()
+
+    def remote(src, dst, send, recv, target):
+        return pltpu.make_async_remote_copy(
+            src_ref=src, dst_ref=dst, send_sem=send, recv_sem=recv,
+            device_id={"ffn": target}, device_id_type=MESH,
+        )
+
+    barrier = pltpu.get_barrier_semaphore()
+    zpeers = [lax.rem(z + d, 4) * 8 + lax.rem(me, 8) for d in (1, 2, 3)]
+    for partner in [mate, xnbr, ynbr] + zpeers:
+        pl.semaphore_signal(barrier, inc=1, device_id={"ffn": partner}, device_id_type=MESH)
+
+    row = lax.broadcasted_iota(jnp.int32, (16, LANES), 0)
+    lane = lax.broadcasted_iota(jnp.int32, (16, LANES), 1)
+    labels = jnp.zeros((16, LANES), F32)
+    for t in range(4):
+        for k, ref in enumerate((step_ref, segment_ref, code_ref)):
+            labels = jnp.where((row == t) & (lane == k), ref[t].astype(F32), labels)
+
+    def fold(ref):
+        full = ref[...].astype(F32)
+        return jnp.concatenate([full[:, c * wide:(c + 1) * wide] for c in range(4)], axis=0)
+
+    raw[z, :, 0:LANES] = labels.astype(BF)
+    raw[z, :, LANES:LANES + wide] = fold(x_ref).astype(BF)
+    raw[z, :, LANES + wide:LANES + 2 * wide] = fold(g_ref).astype(BF)
+    pl.semaphore_wait(barrier, 6)
+
+    def upward(s, block):
+        return remote(raw.at[block], raw.at[block], up_send.at[s], up_recv.at[s], me + 8)
+
+    def downward(s, block):
+        return remote(raw.at[block], raw.at[block], dn_send.at[s], dn_recv.at[s], me - 8)
+
+    for s in range(3):
+        @pl.when((z < 3) & (z - s >= 0))
+        def _(s=s):
+            upward(s, z - s).start()
+
+        @pl.when((z > 0) & (z + s <= 3))
+        def _(s=s):
+            downward(s, z + s).start()
+
+        @pl.when(z - 1 - s >= 0)
+        def _(s=s):
+            upward(s, z - 1 - s).wait_recv()
+
+        @pl.when(z + 1 + s <= 3)
+        def _(s=s):
+            downward(s, z + 1 + s).wait_recv()
+
+    mine = core * 4 + x * 2 + y
+    by_y = core * 4 + x * 2 + 1 - y
+    by_x = core * 4 + (1 - x) * 2 + y
+    diag = core * 4 + (1 - x) * 2 + 1 - y
+    flip = 4 - 8 * core
+    xp = pl.ds(0, LANES + features)
+    gp = pl.ds(LANES + features, features)
+
+    pieces = [raw[k].astype(F32) for k in range(4)]
+    rows[mine, :, 0:LANES] = jnp.concatenate(
+        [piece[0:4, 0:LANES] for piece in pieces], axis=0
+    ).astype(BF)
+    for a in range(2):
+        for c in range(4):
+            lo = LANES + a * wide
+            out = LANES + a * features + c * wide
+            rows[mine, :, out:out + wide] = jnp.concatenate(
+                [piece[4 * c:4 * c + 4, lo:lo + wide] for piece in pieces], axis=0
+            ).astype(BF)
+
+    def plane(i, block, columns, target):
+        view = rows.at[block] if columns is None else rows.at[block, :, columns]
+        return remote(view, view, l_send.at[i], l_recv.at[i], target)
+
+    sends = [
+        plane(0, mine, xp, ynbr),
+        plane(1, mine, gp, xnbr),
+        plane(2, mine, xp, xnbr),
+        plane(3, mine, gp, ynbr),
+        plane(4, mine, None, mate),
+        plane(5, by_y, xp, xnbr),
+        plane(6, by_x, gp, ynbr),
+        plane(7, by_x, None, mate),
+        plane(8, by_y, None, mate),
+        plane(9, diag, None, mate),
+    ]
+    takes = [
+        plane(0, by_y, xp, ynbr),
+        plane(1, by_x, gp, xnbr),
+        plane(2, by_x, xp, xnbr),
+        plane(3, by_y, gp, ynbr),
+        plane(4, mine + flip, None, mate),
+        plane(5, diag, xp, xnbr),
+        plane(6, diag, gp, ynbr),
+        plane(7, by_x + flip, None, mate),
+        plane(8, by_y + flip, None, mate),
+        plane(9, diag + flip, None, mate),
+    ]
+    for i in range(5):
+        sends[i].start()
+    takes[0].wait_recv()
+    sends[5].start()
+    takes[1].wait_recv()
+    sends[6].start()
+    takes[2].wait_recv()
+    sends[7].start()
+    takes[3].wait_recv()
+    sends[8].start()
+    takes[5].wait_recv()
+    takes[6].wait_recv()
+    sends[9].start()
+    for i in (4, 7, 8, 9):
+        takes[i].wait_recv()
+
+    tokens = 8 * 16
+    tags = rows[:, :, 0:LANES].reshape(tokens, LANES)
+    pick = (
+        lax.broadcasted_iota(jnp.int32, (16, LANES), 0)
+        == lax.broadcasted_iota(jnp.int32, (16, LANES), 1)
+    ).astype(F32).astype(BF)
+    across = contract_last(pick, tags)
+    down = tags.astype(F32)
+    gap = across[0:1, :] - down[:, 0:1]
+    same = across[1:2, :] == down[:, 1:2]
+    decay = jnp.where(same & (gap >= 0.0), jnp.exp(gap * math.log(0.75)), 0.0)
+    total = jnp.sum(decay * across[2:3, :], axis=1, keepdims=True)
+    count = jnp.sum(jnp.where(same, 1.0, 0.0), axis=1, keepdims=True)
+    advantage = total / (8.0 * jnp.sqrt(count))
+
+    for load in loads:
+        load.wait()
+    gate_pre = jnp.zeros((tokens, gate_w.shape[1]), F32)
+    up_pre = jnp.zeros((tokens, gate_w.shape[1]), F32)
+    hidden_grad = jnp.zeros((tokens, gate_w.shape[1]), F32)
+    for c in range(4):
+        cols = slice(c * wide, (c + 1) * wide)
+        xs = rows[:, :, LANES + c * wide:LANES + (c + 1) * wide].reshape(tokens, wide)
+        x_out[:, cols] = xs
+        gate_pre += jnp.dot(xs, gate_w[cols, :], preferred_element_type=F32)
+        up_pre += jnp.dot(xs, up_w[cols, :], preferred_element_type=F32)
+        lo = LANES + features + c * wide
+        gs = rows[:, :, lo:lo + wide].reshape(tokens, wide)
+        weighted = (advantage * gs.astype(F32)).astype(BF)
+        weighted_out[:, cols] = weighted
+        hidden_grad += contract_last(weighted, down_w[:, cols])
+    sigma = 1.0 / (1.0 + jnp.exp(-gate_pre))
+    hidden_out[...] = (gate_pre * sigma * up_pre).astype(BF)
+    up_delta = (hidden_grad * gate_pre * sigma).astype(BF)
+    gate_delta = (hidden_grad * up_pre * sigma * (1.0 + gate_pre * (1.0 - sigma))).astype(BF)
+    up_delta_out[...] = up_delta
+    gate_delta_out[...] = gate_delta
+
+    for k in range(4):
+        cols = slice(k * wide, (k + 1) * wide)
+        share = contract_last(gate_delta, gate_w[cols, :]) + contract_last(up_delta, up_w[cols, :])
+        part[k] = share.reshape(8, 16, wide)
+        core_out[k] = part[k, pl.ds((1 - core) * 4, 4)].astype(BF)
+        remote(core_out.at[k], core_in.at[k], core_send.at[k], core_recv.at[k], mate).start()
+
+    def first(k):
+        return remote(
+            first_out.at[k], first_in.at[k], first_send.at[k], first_recv.at[k],
+            xnbr if k % 2 == 0 else ynbr,
+        )
+
+    def second(k):
+        return remote(
+            second_out.at[k], second_in.at[k], second_send.at[k], second_recv.at[k],
+            ynbr if k % 2 == 0 else xnbr,
+        )
+
+    for k in range(4):
+        remote(core_out.at[k], core_in.at[k], core_send.at[k], core_recv.at[k], mate).wait_recv()
+        sums[k] = part[k, pl.ds(core * 4, 4)] + core_in[k].astype(F32)
+        for j in range(2):
+            other = (1 - x) * 2 + j if k % 2 == 0 else j * 2 + 1 - y
+            first_out[k, j] = sums[k, other].astype(BF)
+        first(k).start()
+    for k in range(4):
+        first(k).wait_recv()
+        for j in range(2):
+            own = x * 2 + j if k % 2 == 0 else j * 2 + y
+            halves[k, j] = sums[k, own] + first_in[k, j].astype(F32)
+        side = y if k % 2 == 0 else x
+        second_out[k] = halves[k, 1 - side].astype(BF)
+        second(k).start()
+    for k in range(4):
+        second(k).wait_recv()
+        side = y if k % 2 == 0 else x
+        blocks[k] = halves[k, side] + second_in[k].astype(F32)
+    stripes = [blocks[k] for k in range(4)]
+    for zz in range(4):
+        folded = jnp.concatenate([stripe[4 * zz:4 * zz + 4, :] for stripe in stripes], axis=0)
+        last_keep[zz] = folded
+        last_out[zz] = folded.astype(BF)
+
+    def last(d):
+        there = lax.rem(z + d, 4)
+        return remote(
+            last_out.at[there], last_in.at[d - 1], z_send.at[d - 1], z_recv.at[d - 1],
+            there * 8 + lax.rem(me, 8),
+        )
+
+    for d in (1, 2, 3):
+        last(d).start()
+    for d in (1, 2, 3):
+        last(d).wait_recv()
+    final = last_keep[z] + last_in[0].astype(F32) + last_in[1].astype(F32) + last_in[2].astype(F32)
+    for k in range(4):
+        input_grad_ref[:, k * wide:(k + 1) * wide] = final[4 * k:4 * k + 4, :].astype(BF)
+
+    for s in range(3):
+        @pl.when((z < 3) & (z - s >= 0))
+        def _(s=s):
+            upward(s, z - s).wait_send()
+
+        @pl.when((z > 0) & (z + s <= 3))
+        def _(s=s):
+            downward(s, z + s).wait_send()
+    for send in sends:
+        send.wait_send()
+    for k in range(4):
+        remote(core_out.at[k], core_in.at[k], core_send.at[k], core_recv.at[k], mate).wait_send()
+        first(k).wait_send()
+        second(k).wait_send()
+    for d in (1, 2, 3):
+        last(d).wait_send()
+
+
+def fused(
+    hidden_in, out_grad, step_ids, segment_ids, advantage_codes, gate_weight, up_weight, down_weight
+):
+    features, units = gate_weight.shape
+    tokens = 32 * hidden_in.shape[0]
+    wide = features // 4
+    vmem = pl.BlockSpec(memory_space=pltpu.VMEM)
+    smem = pl.BlockSpec(memory_space=pltpu.SMEM)
+    hbm = pl.BlockSpec(memory_space=pl.ANY)
+    dma = pltpu.SemaphoreType.DMA
+    input_grad, inputs_all, weighted, hidden, gate_delta, up_delta = pl.pallas_call(
+        gather_kernel,
+        out_shape=(
+            jax.ShapeDtypeStruct(hidden_in.shape, BF),
+            jax.ShapeDtypeStruct((tokens, features), BF),
+            jax.ShapeDtypeStruct((tokens, features), BF),
+            jax.ShapeDtypeStruct((tokens, units), BF),
+            jax.ShapeDtypeStruct((tokens, units), BF),
+            jax.ShapeDtypeStruct((tokens, units), BF),
+        ),
+        in_specs=[vmem, vmem, smem, smem, smem, hbm, hbm, hbm],
+        out_specs=(vmem,) * 6,
+        scratch_shapes=[
+            pltpu.VMEM((features, units), BF),
+            pltpu.VMEM((features, units), BF),
+            pltpu.VMEM((units, features), BF),
+            pltpu.VMEM((4, 16, LANES + 2 * wide), BF),
+            pltpu.VMEM((8, 16, LANES + 2 * features), BF),
+            pltpu.VMEM((4, 8, 16, wide), F32),
+            pltpu.VMEM((4, 4, 16, wide), BF),
+            pltpu.VMEM((4, 4, 16, wide), BF),
+            pltpu.VMEM((4, 4, 16, wide), F32),
+            pltpu.VMEM((4, 2, 16, wide), BF),
+            pltpu.VMEM((4, 2, 16, wide), BF),
+            pltpu.VMEM((4, 2, 16, wide), F32),
+            pltpu.VMEM((4, 16, wide), BF),
+            pltpu.VMEM((4, 16, wide), BF),
+            pltpu.VMEM((4, 16, wide), F32),
+            pltpu.VMEM((4, 16, wide), F32),
+            pltpu.VMEM((4, 16, wide), BF),
+            pltpu.VMEM((3, 16, wide), BF),
+            dma((3,)),
+            dma((3,)), dma((3,)), dma((3,)), dma((3,)),
+            dma((10,)), dma((10,)),
+            dma((4,)), dma((4,)), dma((4,)), dma((4,)), dma((4,)), dma((4,)),
+            dma((3,)), dma((3,)),
+        ],
+        compiler_params=pltpu.CompilerParams(
+            collective_id=0, has_side_effects=True, vmem_limit_bytes=48 * 1024 * 1024
+        ),
+        cost_estimate=pl.CostEstimate(
+            flops=10 * tokens * features * units, bytes_accessed=6 * features * units, transcendentals=0
+        ),
+        name="gather_and_sum",
+    )(
+        hidden_in, out_grad, step_ids, segment_ids, advantage_codes,
+        gate_weight, up_weight, down_weight,
+    )
+    down_grad = contract_first(hidden, weighted).astype(BF)
+    gate_grad = contract_first(inputs_all, gate_delta).astype(BF)
+    up_grad = contract_first(inputs_all, up_delta).astype(BF)
+    return (input_grad, gate_grad, up_grad, down_grad)
 
 
 def local(
@@ -75,4 +402,5 @@
         P(("groups", "mp"), "ffn"),
         P(("groups", "ffn"), "mp"),
     )
-    return jax.shard_map(local, mesh=mesh, in_specs=in_specs, out_specs=out_specs, check_vma=False)
+    whole = mesh.shape["groups"] == 1 and mesh.shape["mp"] == 1 and mesh.shape["ffn"] == 32
+    return jax.shard_map(fused if whole else local, mesh=mesh, in_specs=in_specs, out_specs=out_specs, check_vma=False)

time: 204 us -> 59 us (0.29)
  blocking collectives: 104 us -> 0 us
  waiting for transfers between devices: 66.7 us -> 0 us
  Pallas kernels: 0 us -> 43.6 us
  between operations: 14.1 us -> 0.69 us
  matrix products: 13.8 us -> 5.7 us
  local copies, waits for them, and re-layouts: 4.61 us -> 8.73 us
    all_gather x2 -> x0, waiting for transfers between devices: 65.3 us -> none  [the longest x1 51.4 us: local(): lax.all_gather(out_grad, 'ffn', axis=0, tiled=True)]
    unnamed x1 -> x0, blocking collectives: 60.3 us -> none
    pallas_call x0 -> x1, Pallas kernels: none -> 43.6 us  [fused(): pl.pallas_call(gather_kernel, out_shape=(jax.ShapeDtypeStruct(hidden_in.s...]
    all_gather x1 -> x0, blocking collectives: 43.4 us -> none  [local(): lax.all_gather(jnp.stack([step_ids, segment_ids, advantage_codes]), 'ffn'...]
    dot_general x6 -> x0, matrix products: 8.17 us -> none  [the longest x3 5.14 us: contract_last(): lax.dot_general(left, right, (((1,), (1,)), ((), ())), preferred_element_...]
    unnamed x9 -> x15, local copies, waits for them, and re-layouts: 1.51 us -> 8.73 us
    convert_element_type x2 -> x0, local copies, waits for them, and re-layouts: 3.09 us -> none  [the longest x1 2.45 us: local(): grads_all.astype(jnp.float32)]
  transfers between devices with their start and end apart: 2 -> 0, of which waited for: 2 -> 0; matrix products, arithmetic and copies ran while one was open for 3% -> 0% of each run, Pallas kernels for 0% -> 0%
where the time goes in v1:
time: 59 us; the launch traced here: 58.8 us
  Pallas kernels  43.6 us (74%)
  local copies, waits for them, and re-layouts  8.73 us (15%)
  matrix products  5.7 us (10%)
  between operations  0.69 us (1%)
    pallas_call x1, Pallas kernels, fused(): pl.pallas_call(gather_kernel, out_shape=(jax.ShapeDtypeStruct(hidden_in.s...  43.6 us
    unnamed x15, local copies, waits for them, and re-layouts  8.73 us
    dot_general x3, matrix products, contract_first(): lax.dot_general(left, right, (((0,), (0,)), ((), ())), preferred_element_...  5.7 us

profile of v1, /device:TPU:0, one launch (start us, length us, event | category | flops | bytes accessed | tf_op | source)
XLA Modules:
  0.0 58.8 jit_solution(15060664231592698876)
XLA Ops:
  0.6 4.0 %copy.12.gate_hbm = bf16[4096,224]{1,0:T(8,128)(2,1)} copy(bf16[4096,224]{0,1:T(8,128)(2,1)} %param.13) | data formatting | bytes 3670016 | tf_op args[5]
  4.6 0.0 copy-start
  4.6 0.0 copy-start.1
  4.6 0.0 copy-start.2
  4.6 0.0 copy-start.3
  4.6 0.0 copy-start.4
  4.6 0.0 copy-start.5
  4.7 4.1 %copy.13.up_hbm = bf16[4096,224]{1,0:T(8,128)(2,1)} copy(bf16[4096,224]{0,1:T(8,128)(2,1)} %param.14) | data formatting | bytes 3670016 | tf_op args[6]
  8.8 0.0 copy-done
  8.8 0.0 copy-done.1
  8.8 0.0 copy-done.2
  8.8 0.0 copy-done.3
  8.8 0.0 copy-done.4
  8.8 0.0 copy-done.5
  8.8 43.6 %gather_and_sum.1 = (bf16[4,4096]{1,0:T(4,128)(2,1)S(1)}, bf16[128,4096]{1,0:T(8,128)(2,1)S(1)}, bf16[128,4096]{1,0:T(8,128)(2,1)S(1)}, bf16[128,224]{1,0:T(8,12...) custom-call(bf16[4,4096]{1,0:T(4,128)(2,1)S(1)} %copy-done.1, bf16[4,4096]{1,0:T(4,128)(2,1)S(1)} %copy-done.2, ...), custom_call_target="tpu_custom_call" | custom-call | flops 1174405120 | bytes 5505024 | tf_op jit(solution)/shard_map/gather_and_sum/pallas_call | solution.py:304
  52.5 1.9 %convolution_convert_fusion.2 = bf16[4096,224]{0,1:T(8,128)(2,1)} fusion(bf16[128,4096]{1,0:T(8,128)(2,1)S(1)} %get-tuple-element.11, bf16[128,224]{1,0:T(8,128)(2,1)S(1)} %get-tuple-element.12), kind=kOutput, calls=%fused_computation.2 | convolution fusion | flops 235798528 | bytes 2940928 | tf_op jit(solution)/shard_map/dot_general | solution.py:28
  54.4 1.9 %convolution_convert_fusion.1 = bf16[4096,224]{0,1:T(8,128)(2,1)} fusion(bf16[128,4096]{1,0:T(8,128)(2,1)S(1)} %get-tuple-element.11, bf16[128,224]{1,0:T(8,128)(2,1)S(1)} %get-tuple-element.13), kind=kOutput, calls=%fused_computation.1 | convolution fusion | flops 235798528 | bytes 2940928 | tf_op jit(solution)/shard_map/dot_general | solution.py:28
  56.3 1.9 %convolution_convert_fusion = bf16[224,4096]{1,0:T(8,128)(2,1)} fusion(bf16[128,224]{1,0:T(8,128)(2,1)S(1)} %get-tuple-element.14, bf16[128,4096]{1,0:T(8,128)(2,1)S(1)} %get-tuple-element.15), kind=kOutput, calls=%fused_computation | convolution fusion | flops 235798528 | bytes 2940928 | tf_op jit(solution)/shard_map/dot_general | solution.py:28
  58.2 0.6 %copy.15 = bf16[4,4096]{1,0:T(4,128)(2,1)} copy(bf16[4,4096]{1,0:T(4,128)(2,1)S(1)} %get-tuple-element.20) | data formatting | bytes 65536
Async XLA Ops:
  4.6 4.1 %copy-start = (bf16[224,4096]{1,0:T(8,128)(2,1)S(1)}, bf16[224,4096]{1,0:T(8,128)(2,1)}, u32[]{:S(2)}) copy-start(bf16[224,4096]{1,0:T(8,128)(2,1)} %down_hbm.1) | copy-start | bytes 5505028
  4.6 4.1 %copy-start.1 = (bf16[4,4096]{1,0:T(4,128)(2,1)S(1)}, bf16[4,4096]{1,0:T(4,128)(2,1)}, u32[]{:S(2)}) copy-start(bf16[4,4096]{1,0:T(4,128)(2,1)} %x_ref.1) | copy-start | bytes 98308
  4.6 4.1 %copy-start.2 = (bf16[4,4096]{1,0:T(4,128)(2,1)S(1)}, bf16[4,4096]{1,0:T(4,128)(2,1)}, u32[]{:S(2)}) copy-start(bf16[4,4096]{1,0:T(4,128)(2,1)} %g_ref.1) | copy-start | bytes 98308
  4.6 4.1 %copy-start.3 = (s32[4]{0:T(128)S(1)}, s32[4]{0:T(128)}, u32[]{:S(2)}) copy-start(s32[4]{0:T(128)} %step_ref.1) | copy-start | bytes 52
  4.6 4.2 %copy-start.4 = (s32[4]{0:T(128)S(1)}, s32[4]{0:T(128)}, u32[]{:S(2)}) copy-start(s32[4]{0:T(128)} %segment_ref.1) | copy-start | bytes 52
  4.6 4.1 %copy-start.5 = (s32[4]{0:T(128)S(1)}, s32[4]{0:T(128)}, u32[]{:S(2)}) copy-start(s32[4]{0:T(128)} %code_ref.1) | copy-start | bytes 52

commit v2 on v1

--- a/solution.py
+++ b/solution.py
@@ -38,8 +38,8 @@
 
 def gather_kernel(
     x_ref, g_ref, step_ref, segment_ref, code_ref, gate_hbm, up_hbm, down_hbm,
-    input_grad_ref, x_out, weighted_out, hidden_out, gate_delta_out, up_delta_out,
-    gate_w, up_w, down_w, raw, rows, part, core_out, core_in, sums, first_out, first_in,
+    input_grad_ref, gate_grad_ref, up_grad_ref, down_grad_ref,
+    gate_w, up_w, down_w, weighted_all, raw, rows, part, core_out, core_in, sums, first_out, first_in,
     halves, second_out, second_in, blocks, last_keep, last_out, last_in,
     weight_sem, up_send, up_recv, dn_send, dn_recv, l_send, l_recv,
     core_send, core_recv, first_send, first_recv, second_send, second_recv, z_send, z_recv,
@@ -193,30 +193,28 @@
 
     for load in loads:
         load.wait()
-    gate_pre = jnp.zeros((tokens, gate_w.shape[1]), F32)
-    up_pre = jnp.zeros((tokens, gate_w.shape[1]), F32)
-    hidden_grad = jnp.zeros((tokens, gate_w.shape[1]), F32)
+    gate_pre = jnp.zeros((tokens, gate_w.shape[0]), F32)
+    up_pre = jnp.zeros((tokens, gate_w.shape[0]), F32)
+    hidden_grad = jnp.zeros((tokens, gate_w.shape[0]), F32)
     for c in range(4):
         cols = slice(c * wide, (c + 1) * wide)
         xs = rows[:, :, LANES + c * wide:LANES + (c + 1) * wide].reshape(tokens, wide)
-        x_out[:, cols] = xs
-        gate_pre += jnp.dot(xs, gate_w[cols, :], preferred_element_type=F32)
-        up_pre += jnp.dot(xs, up_w[cols, :], preferred_element_type=F32)
+        gate_pre += contract_last(xs, gate_w[:, cols])
+        up_pre += contract_last(xs, up_w[:, cols])
         lo = LANES + features + c * wide
         gs = rows[:, :, lo:lo + wide].reshape(tokens, wide)
         weighted = (advantage * gs.astype(F32)).astype(BF)
-        weighted_out[:, cols] = weighted
+        weighted_all[:, cols] = weighted
         hidden_grad += contract_last(weighted, down_w[:, cols])
     sigma = 1.0 / (1.0 + jnp.exp(-gate_pre))
-    hidden_out[...] = (gate_pre * sigma * up_pre).astype(BF)
+    hidden = (gate_pre * sigma * up_pre).astype(BF)
     up_delta = (hidden_grad * gate_pre * sigma).astype(BF)
     gate_delta = (hidden_grad * up_pre * sigma * (1.0 + gate_pre * (1.0 - sigma))).astype(BF)
-    up_delta_out[...] = up_delta
-    gate_delta_out[...] = gate_delta
 
     for k in range(4):
         cols = slice(k * wide, (k + 1) * wide)
-        share = contract_last(gate_delta, gate_w[cols, :]) + contract_last(up_delta, up_w[cols, :])
+        share = jnp.dot(gate_delta, gate_w[:, cols], preferred_element_type=F32)
+        share += jnp.dot(up_delta, up_w[:, cols], preferred_element_type=F32)
         part[k] = share.reshape(8, 16, wide)
         core_out[k] = part[k, pl.ds((1 - core) * 4, 4)].astype(BF)
         remote(core_out.at[k], core_in.at[k], core_send.at[k], core_recv.at[k], mate).start()
@@ -233,6 +231,15 @@
             ynbr if k % 2 == 0 else xnbr,
         )
 
+    def weight_grad(out, delta, by_tokens):
+        for c in range(4):
+            cols = slice(c * wide, (c + 1) * wide)
+            out[:, cols] = contract_first(delta, by_tokens(c)).astype(BF)
+
+    def inputs_of(c):
+        return rows[:, :, LANES + c * wide:LANES + (c + 1) * wide].reshape(tokens, wide)
+
+    weight_grad(gate_grad_ref, gate_delta, inputs_of)
     for k in range(4):
         remote(core_out.at[k], core_in.at[k], core_send.at[k], core_recv.at[k], mate).wait_recv()
         sums[k] = part[k, pl.ds(core * 4, 4)] + core_in[k].astype(F32)
@@ -240,6 +247,7 @@
             other = (1 - x) * 2 + j if k % 2 == 0 else j * 2 + 1 - y
             first_out[k, j] = sums[k, other].astype(BF)
         first(k).start()
+    weight_grad(up_grad_ref, up_delta, inputs_of)
     for k in range(4):
         first(k).wait_recv()
         for j in range(2):
@@ -248,6 +256,7 @@
         side = y if k % 2 == 0 else x
         second_out[k] = halves[k, 1 - side].astype(BF)
         second(k).start()
+    weight_grad(down_grad_ref, hidden, lambda c: weighted_all[:, c * wide:(c + 1) * wide])
     for k in range(4):
         second(k).wait_recv()
         side = y if k % 2 == 0 else x
@@ -299,24 +308,23 @@
     wide = features // 4
     vmem = pl.BlockSpec(memory_space=pltpu.VMEM)
     smem = pl.BlockSpec(memory_space=pltpu.SMEM)
-    hbm = pl.BlockSpec(memory_space=pl.ANY)
+    hbm = pl.BlockSpec(memory_space=pltpu.HBM)
     dma = pltpu.SemaphoreType.DMA
-    input_grad, inputs_all, weighted, hidden, gate_delta, up_delta = pl.pallas_call(
+    input_grad, gate_grad, up_grad, down_grad = pl.pallas_call(
         gather_kernel,
         out_shape=(
             jax.ShapeDtypeStruct(hidden_in.shape, BF),
-            jax.ShapeDtypeStruct((tokens, features), BF),
-            jax.ShapeDtypeStruct((tokens, features), BF),
-            jax.ShapeDtypeStruct((tokens, units), BF),
-            jax.ShapeDtypeStruct((tokens, units), BF),
-            jax.ShapeDtypeStruct((tokens, units), BF),
+            jax.ShapeDtypeStruct((units, features), BF),
+            jax.ShapeDtypeStruct((units, features), BF),
+            jax.ShapeDtypeStruct((units, features), BF),
         ),
         in_specs=[vmem, vmem, smem, smem, smem, hbm, hbm, hbm],
-        out_specs=(vmem,) * 6,
+        out_specs=(vmem,) * 4,
         scratch_shapes=[
-            pltpu.VMEM((features, units), BF),
-            pltpu.VMEM((features, units), BF),
             pltpu.VMEM((units, features), BF),
+            pltpu.VMEM((units, features), BF),
+            pltpu.VMEM((units, features), BF),
+            pltpu.VMEM((tokens, features), BF),
             pltpu.VMEM((4, 16, LANES + 2 * wide), BF),
             pltpu.VMEM((8, 16, LANES + 2 * features), BF),
             pltpu.VMEM((4, 8, 16, wide), F32),
@@ -339,7 +347,7 @@
             dma((3,)), dma((3,)),
         ],
         compiler_params=pltpu.CompilerParams(
-            collective_id=0, has_side_effects=True, vmem_limit_bytes=48 * 1024 * 1024
+            collective_id=0, has_side_effects=True, vmem_limit_bytes=36 * 1024 * 1024
         ),
         cost_estimate=pl.CostEstimate(
             flops=10 * tokens * features * units, bytes_accessed=6 * features * units, transcendentals=0
@@ -347,12 +355,9 @@
         name="gather_and_sum",
     )(
         hidden_in, out_grad, step_ids, segment_ids, advantage_codes,
-        gate_weight, up_weight, down_weight,
-    )
-    down_grad = contract_first(hidden, weighted).astype(BF)
-    gate_grad = contract_first(inputs_all, gate_delta).astype(BF)
-    up_grad = contract_first(inputs_all, up_delta).astype(BF)
-    return (input_grad, gate_grad, up_grad, down_grad)
+        gate_weight.T, up_weight.T, down_weight,
+    )
+    return (input_grad, gate_grad.T, up_grad.T, down_grad)
 
 
 def local(

time: 59 us -> 57.5 us (0.975)
  matrix products: 5.7 us -> 0 us
  local copies, waits for them, and re-layouts: 8.73 us -> 12.3 us
  Pallas kernels: 43.6 us -> 44.2 us
    dot_general x3 -> x0, matrix products: 5.7 us -> none  [contract_first(): lax.dot_general(left, right, (((0,), (0,)), ((), ())), preferred_element_...]
    unnamed x15 -> x20, local copies, waits for them, and re-layouts: 8.73 us -> 12.3 us
where the time goes in v2:
time: 57.5 us; the launch traced here: 57.1 us
  Pallas kernels  44.2 us (77%)
  local copies, waits for them, and re-layouts  12.3 us (21%)
  between operations  0.66 us (1%)
    pallas_call x1, Pallas kernels, fused(): pl.pallas_call(gather_kernel, out_shape=(jax.ShapeDtypeStruct(hidden_in.s...  44.2 us
    unnamed x20, local copies, waits for them, and re-layouts  12.3 us

profile of v2, /device:TPU:0, one launch (start us, length us, event | category | flops | bytes accessed | tf_op | source)
XLA Modules:
  0.0 57.1 jit_solution(10799800541096157081)
XLA Ops:
  0.6 0.0 copy-start
  0.6 1.5 %copy-done = bf16[4096,224]{0,1:T(8,128)(2,1)S(1)} copy-done((bf16[4096,224]{0,1:T(8,128)(2,1)S(1)}, bf16[4096,224]{0,1:T(8,128)(2,1)}, u32[]{:S(2)}) %copy-start) | copy-done | bytes 1835032
  2.1 0.0 copy-start.1
  2.1 1.5 %copy-done.1 = bf16[4096,224]{0,1:T(8,128)(2,1)S(1)} copy-done((bf16[4096,224]{0,1:T(8,128)(2,1)S(1)}, bf16[4096,224]{0,1:T(8,128)(2,1)}, u32[]{:S(2)}) %copy-start.1) | copy-done | bytes 1835032
  3.6 0.0 copy-start.2
  3.6 1.5 %copy-done.2 = bf16[224,4096]{1,0:T(8,128)(2,1)S(1)} copy-done((bf16[224,4096]{1,0:T(8,128)(2,1)S(1)}, bf16[224,4096]{1,0:T(8,128)(2,1)}, u32[]{:S(2)}) %copy-start.2) | copy-done | bytes 1835032
  5.1 0.0 copy-start.3
  5.1 0.8 %copy-done.3 = bf16[4,4096]{1,0:T(4,128)(2,1)S(1)} copy-done((bf16[4,4096]{1,0:T(4,128)(2,1)S(1)}, bf16[4,4096]{1,0:T(4,128)(2,1)}, u32[]{:S(2)}) %copy-start.3) | copy-done | bytes 32792
  5.9 0.0 copy-start.4
  5.9 0.8 %copy-done.4 = bf16[4,4096]{1,0:T(4,128)(2,1)S(1)} copy-done((bf16[4,4096]{1,0:T(4,128)(2,1)S(1)}, bf16[4,4096]{1,0:T(4,128)(2,1)}, u32[]{:S(2)}) %copy-start.4) | copy-done | bytes 32792
  6.7 0.0 copy-start.5
  6.7 0.7 %copy-done.5 = s32[4]{0:T(128)S(1)} copy-done((s32[4]{0:T(128)S(1)}, s32[4]{0:T(128)}, u32[]{:S(2)}) %copy-start.5) | copy-done | bytes 40
  7.3 0.0 copy-start.6
  7.3 0.7 %copy-done.6 = s32[4]{0:T(128)S(1)} copy-done((s32[4]{0:T(128)S(1)}, s32[4]{0:T(128)}, u32[]{:S(2)}) %copy-start.6) | copy-done | bytes 40
  8.0 0.0 copy-start.7
  8.0 0.7 %copy-done.7 = s32[4]{0:T(128)S(1)} copy-done((s32[4]{0:T(128)S(1)}, s32[4]{0:T(128)}, u32[]{:S(2)}) %copy-start.7) | copy-done | bytes 40
  8.6 44.2 %gather_and_sum.1 = (bf16[4,4096]{1,0:T(4,128)(2,1)S(1)}, bf16[224,4096]{1,0:T(8,128)(2,1)S(1)}, bf16[224,4096]{1,0:T(8,128)(2,1)S(1)}, bf16[224,4096]{1,0:T(8,128)(2,1)S(1)}) custom-call(bf16[4,4096]{1,0:T(4,128)(2,1)S(1)} %copy-done.3, bf16[4,4096]{1,0:T(4,128)(2,1)S(1)} %copy-done.4, s32[4]{0:T(128)S(1)} %copy-done.5, s32[4]{0:T(128)S(1)} %copy-done.6, ...), custom_call_target="tpu_custom_call" | custom-call | flops 1174405120 | bytes 5505024 | tf_op jit(solution)/shard_map/gather_and_sum/pallas_call | solution.py:313
  52.8 0.6 %copy.16 = bf16[4,4096]{1,0:T(4,128)(2,1)} copy(bf16[4,4096]{1,0:T(4,128)(2,1)S(1)} %get-tuple-element.16) | data formatting | bytes 65536
  53.4 1.2 %copy.17 = bf16[4096,224]{0,1:T(8,128)(2,1)} copy(bf16[4096,224]{0,1:T(8,128)(2,1)S(1)} %bitcast.5) | data formatting | bytes 3670016
  54.7 1.2 %copy.18 = bf16[4096,224]{0,1:T(8,128)(2,1)} copy(bf16[4096,224]{0,1:T(8,128)(2,1)S(1)} %bitcast.4) | data formatting | bytes 3670016
  55.9 1.2 %copy.19 = bf16[224,4096]{1,0:T(8,128)(2,1)} copy(bf16[224,4096]{1,0:T(8,128)(2,1)S(1)} %get-tuple-element.19) | data formatting | bytes 3670016
Async XLA Ops:
  0.6 1.5 %copy-start = (bf16[4096,224]{0,1:T(8,128)(2,1)S(1)}, bf16[4096,224]{0,1:T(8,128)(2,1)}, u32[]{:S(2)}) copy-start(bf16[4096,224]{0,1:T(8,128)(2,1)} %param.13) | copy-start | bytes 5505028
  2.1 1.5 %copy-start.1 = (bf16[4096,224]{0,1:T(8,128)(2,1)S(1)}, bf16[4096,224]{0,1:T(8,128)(2,1)}, u32[]{:S(2)}) copy-start(bf16[4096,224]{0,1:T(8,128)(2,1)} %param.14) | copy-start | bytes 5505028
  3.6 1.5 %copy-start.2 = (bf16[224,4096]{1,0:T(8,128)(2,1)S(1)}, bf16[224,4096]{1,0:T(8,128)(2,1)}, u32[]{:S(2)}) copy-start(bf16[224,4096]{1,0:T(8,128)(2,1)} %down_hbm.1) | copy-start | bytes 5505028
  5.1 0.8 %copy-start.3 = (bf16[4,4096]{1,0:T(4,128)(2,1)S(1)}, bf16[4,4096]{1,0:T(4,128)(2,1)}, u32[]{:S(2)}) copy-start(bf16[4,4096]{1,0:T(4,128)(2,1)} %x_ref.1) | copy-start | bytes 98308
  5.9 0.8 %copy-start.4 = (bf16[4,4096]{1,0:T(4,128)(2,1)S(1)}, bf16[4,4096]{1,0:T(4,128)(2,1)}, u32[]{:S(2)}) copy-start(bf16[4,4096]{1,0:T(4,128)(2,1)} %g_ref.1) | copy-start | bytes 98308
  6.7 0.7 %copy-start.5 = (s32[4]{0:T(128)S(1)}, s32[4]{0:T(128)}, u32[]{:S(2)}) copy-start(s32[4]{0:T(128)} %step_ref.1) | copy-start | bytes 52
  7.3 0.7 %copy-start.6 = (s32[4]{0:T(128)S(1)}, s32[4]{0:T(128)}, u32[]{:S(2)}) copy-start(s32[4]{0:T(128)} %segment_ref.1) | copy-start | bytes 52
  8.0 0.7 %copy-start.7 = (s32[4]{0:T(128)S(1)}, s32[4]{0:T(128)}, u32[]{:S(2)}) copy-start(s32[4]{0:T(128)} %code_ref.1) | copy-start | bytes 52

commit v3 on v0

--- a/solution.py
+++ b/solution.py
@@ -3,6 +3,8 @@
 import jax
 import jax.numpy as jnp
 from jax import lax
+from jax.experimental import pallas as pl
+from jax.experimental.pallas import tpu as pltpu
 from jax.sharding import PartitionSpec as P
 
 
@@ -26,6 +28,355 @@
     return lax.dot_general(
         left, right, (((0,), (0,)), ((), ())), preferred_element_type=jnp.float32
     )
+
+
+BF = jnp.bfloat16
+F32 = jnp.float32
+MESH = pl.DeviceIdType.MESH
+LANES = 128
+
+
+def gather_kernel(
+    x_hbm, g_hbm, step_hbm, segment_hbm, code_hbm, gate_hbm, up_hbm, down_hbm,
+    input_grad_ref, gate_grad_ref, up_grad_ref, down_grad_ref,
+    gate_w, up_w, down_w, weighted_all, x_ref, g_ref, step_ref, segment_ref, code_ref,
+    raw, rows, core_out, core_in, sums, first_out, first_in,
+    halves, second_out, second_in, blocks, last_keep, last_out, last_in,
+    load_sem, za_send, za_recv, x_send, x_recv, y_send, y_recv, fx_send, fx_recv, fy_send, fy_recv,
+    m_send, m_recv,
+    core_send, core_recv, first_send, first_recv, second_send, second_recv, z_send, z_recv,
+):
+    features = x_ref.shape[1]
+    wide = features // 4
+    tokens = 8 * 16
+    me = lax.axis_index("ffn")
+    z = me // 8
+    y = lax.rem(me // 4, 2)
+    x = lax.rem(me // 2, 2)
+    core = lax.rem(me, 2)
+    mate = me + 1 - 2 * core
+    xnbr = me + 2 - 4 * x
+    ynbr = me + 4 - 8 * y
+    ahead = [me] + [lax.rem(z + d, 4) * 8 + lax.rem(me, 8) for d in (1, 2, 3)]
+    behind = [me] + [lax.rem(z + 4 - d, 4) * 8 + lax.rem(me, 8) for d in (1, 2, 3)]
+
+    loads = [
+        pltpu.make_async_copy(src, dst, load_sem.at[i])
+        for i, (src, dst) in enumerate((
+            (x_hbm, x_ref), (g_hbm, g_ref), (step_hbm, step_ref), (segment_hbm, segment_ref),
+            (code_hbm, code_ref), (gate_hbm, gate_w), (up_hbm, up_w), (down_hbm, down_w),
+        ))
+    ]
+    for load in loads:
+        load.start()
+
+    def remote(src, dst, send, recv, target):
+        return pltpu.make_async_remote_copy(
+            src_ref=src, dst_ref=dst, send_sem=send, recv_sem=recv,
+            device_id={"ffn": target}, device_id_type=MESH,
+        )
+
+    barrier = pltpu.get_barrier_semaphore()
+    for partner in [mate, xnbr, ynbr] + ahead[1:]:
+        pl.semaphore_signal(barrier, inc=1, device_id={"ffn": partner}, device_id_type=MESH)
+
+    for load in loads[:5]:
+        load.wait()
+    row = lax.broadcasted_iota(jnp.int32, (16, LANES), 0)
+    lane = lax.broadcasted_iota(jnp.int32, (16, LANES), 1)
+    labels = jnp.zeros((16, LANES), F32)
+    for t in range(4):
+        for k, ref in enumerate((step_ref, segment_ref, code_ref)):
+            labels = jnp.where((row == t) & (lane == k), ref[t].astype(F32), labels)
+
+    def fold(ref):
+        full = ref[...].astype(F32)
+        return jnp.concatenate([full[:, c * wide:(c + 1) * wide] for c in range(4)], axis=0)
+
+    raw[0, 0, :, 0:LANES] = labels.astype(BF)
+    raw[0, 0, :, LANES:LANES + wide] = fold(x_ref).astype(BF)
+    raw[0, 0, :, LANES + wide:LANES + 2 * wide] = fold(g_ref).astype(BF)
+    pl.semaphore_wait(barrier, 6)
+
+    xp = pl.ds(0, LANES + wide)
+    gp = pl.ds(LANES + wide, wide)
+    along_z = [
+        remote(raw.at[0, 0], raw.at[0, d], za_send.at[d - 1], za_recv.at[d - 1], ahead[d])
+        for d in (1, 2, 3)
+    ]
+    to_x = [remote(raw.at[0, d], raw.at[2, d], x_send.at[d], x_recv.at[d], xnbr) for d in range(4)]
+    to_y = [remote(raw.at[0, d], raw.at[1, d], y_send.at[d], y_recv.at[d], ynbr) for d in range(4)]
+    on_x = [
+        remote(raw.at[1, d, :, xp], raw.at[3, d, :, xp], fx_send.at[d], fx_recv.at[d], xnbr)
+        for d in range(4)
+    ]
+    on_y = [
+        remote(raw.at[2, d, :, gp], raw.at[3, d, :, gp], fy_send.at[d], fy_recv.at[d], ynbr)
+        for d in range(4)
+    ]
+
+    def to_mate(slot, half):
+        pieces = pl.ds(2 * half, 2)
+        i = 2 * slot + half
+        return remote(
+            raw.at[slot, pieces], raw.at[4 + slot, pieces], m_send.at[i], m_recv.at[i], mate
+        )
+
+    def onward(d):
+        to_y[d].wait_recv()
+        on_x[d].start()
+        to_x[d].wait_recv()
+        on_y[d].start()
+
+    def unfold(slot):
+        pieces = [raw[slot, d].astype(F32) for d in range(4)]
+        rows[slot, :, 0:LANES] = jnp.concatenate(
+            [piece[0:4, 0:LANES] for piece in pieces], axis=0
+        ).astype(BF)
+        for a in range(2):
+            for c in range(4):
+                lo = LANES + a * wide
+                out = LANES + a * features + c * wide
+                rows[slot, :, out:out + wide] = jnp.concatenate(
+                    [piece[4 * c:4 * c + 4, lo:lo + wide] for piece in pieces], axis=0
+                ).astype(BF)
+
+    for copy in along_z:
+        copy.start()
+    to_y[0].start()
+    to_x[0].start()
+    for d in (1, 2, 3):
+        along_z[d - 1].wait_recv()
+        to_y[d].start()
+        to_x[d].start()
+        if d % 2 == 1:
+            to_mate(0, d // 2).start()
+        onward(d - 1)
+        if d == 2:
+            to_mate(1, 0).start()
+            to_mate(2, 0).start()
+    unfold(0)
+    onward(3)
+    to_mate(1, 1).start()
+    to_mate(2, 1).start()
+    for d in (0, 1):
+        on_x[d].wait_recv()
+        on_y[d].wait_recv()
+    to_mate(3, 0).start()
+    unfold(1)
+    unfold(2)
+    for d in (2, 3):
+        on_x[d].wait_recv()
+        on_y[d].wait_recv()
+    to_mate(3, 1).start()
+    unfold(3)
+    for slot in range(4):
+        to_mate(slot, 0).wait_recv()
+        to_mate(slot, 1).wait_recv()
+        unfold(4 + slot)
+
+    tags = rows[:, :, 0:LANES].reshape(tokens, LANES)
+    pick = (
+        lax.broadcasted_iota(jnp.int32, (16, LANES), 0)
+        == lax.broadcasted_iota(jnp.int32, (16, LANES), 1)
+    ).astype(F32).astype(BF)
+    across = contract_last(pick, tags)
+    down = tags.astype(F32)
+    gap = across[0:1, :] - down[:, 0:1]
+    same = across[1:2, :] == down[:, 1:2]
+    decay = jnp.where(same & (gap >= 0.0), jnp.exp(gap * math.log(0.75)), 0.0)
+    total = jnp.sum(decay * across[2:3, :], axis=1, keepdims=True)
+    count = jnp.sum(jnp.where(same, 1.0, 0.0), axis=1, keepdims=True)
+    advantage = total / (8.0 * jnp.sqrt(count))
+
+    for load in loads[5:]:
+        load.wait()
+
+    def inputs_of(c):
+        return rows[:, :, LANES + c * wide:LANES + (c + 1) * wide].reshape(tokens, wide)
+
+    gate_pre = jnp.zeros((tokens, gate_w.shape[0]), F32)
+    up_pre = jnp.zeros((tokens, gate_w.shape[0]), F32)
+    hidden_grad = jnp.zeros((tokens, gate_w.shape[0]), F32)
+    for c in range(4):
+        cols = slice(c * wide, (c + 1) * wide)
+        xs = inputs_of(c)
+        gate_pre += contract_last(xs, gate_w[:, cols])
+        up_pre += contract_last(xs, up_w[:, cols])
+        lo = LANES + features + c * wide
+        gs = rows[:, :, lo:lo + wide].reshape(tokens, wide)
+        weighted = (advantage * gs.astype(F32)).astype(BF)
+        weighted_all[:, cols] = weighted
+        hidden_grad += contract_last(weighted, down_w[:, cols])
+    sigma = 1.0 / (1.0 + jnp.exp(-gate_pre))
+    hidden = (gate_pre * sigma * up_pre).astype(BF)
+    up_delta = (hidden_grad * gate_pre * sigma).astype(BF)
+    gate_delta = (hidden_grad * up_pre * sigma * (1.0 + gate_pre * (1.0 - sigma))).astype(BF)
+
+    to_core = [
+        remote(core_out.at[k], core_in.at[k], core_send.at[k], core_recv.at[k], mate)
+        for k in range(4)
+    ]
+    first = [
+        remote(
+            first_out.at[k], first_in.at[k], first_send.at[k], first_recv.at[k],
+            xnbr if k % 2 == 0 else ynbr,
+        )
+        for k in range(4)
+    ]
+    second = [
+        remote(
+            second_out.at[k], second_in.at[k], second_send.at[k], second_recv.at[k],
+            ynbr if k % 2 == 0 else xnbr,
+        )
+        for k in range(4)
+    ]
+    last = [
+        remote(last_out.at[d - 1], last_in.at[d - 1], z_send.at[d - 1], z_recv.at[d - 1], behind[d])
+        for d in (1, 2, 3)
+    ]
+    for k in range(4):
+        cols = slice(k * wide, (k + 1) * wide)
+        share = jnp.dot(gate_delta, gate_w[:, cols], preferred_element_type=F32)
+        share += jnp.dot(up_delta, up_w[:, cols], preferred_element_type=F32)
+        share = share.reshape(8, 16, wide)
+        core_out[k] = share[4:8].astype(BF)
+        to_core[k].start()
+        sums[k] = share[0:4]
+
+    def weight_grad(out, delta, by_tokens):
+        for c in range(4):
+            cols = slice(c * wide, (c + 1) * wide)
+            out[:, cols] = contract_first(delta, by_tokens(c)).astype(BF)
+
+    for k in range(4):
+        leave, stay = ((2, 3), (0, 1)) if k % 2 == 0 else ((1, 3), (0, 2))
+        to_core[k].wait_recv()
+        for j in range(2):
+            first_out[k, j] = (sums[k, leave[j]] + core_in[k, leave[j]].astype(F32)).astype(BF)
+        first[k].start()
+        for j in range(2):
+            halves[k, j] = sums[k, stay[j]] + core_in[k, stay[j]].astype(F32)
+    weight_grad(gate_grad_ref, gate_delta, inputs_of)
+    for k in range(4):
+        first[k].wait_recv()
+        second_out[k] = (halves[k, 1] + first_in[k, 1].astype(F32)).astype(BF)
+        second[k].start()
+        blocks[k] = halves[k, 0] + first_in[k, 0].astype(F32)
+    weight_grad(up_grad_ref, up_delta, inputs_of)
+    for k in range(4):
+        second[k].wait_recv()
+    stripes = [blocks[k] + second_in[k].astype(F32) for k in range(4)]
+    for d in (3, 2, 1, 0):
+        folded = jnp.concatenate([stripe[4 * d:4 * d + 4, :] for stripe in stripes], axis=0)
+        if d == 0:
+            last_keep[...] = folded
+        else:
+            last_out[d - 1] = folded.astype(BF)
+            last[d - 1].start()
+    weight_grad(down_grad_ref, hidden, lambda c: weighted_all[:, c * wide:(c + 1) * wide])
+    final = last_keep[...]
+    for d in range(3):
+        last[d].wait_recv()
+        final += last_in[d].astype(F32)
+    for k in range(4):
+        input_grad_ref[:, k * wide:(k + 1) * wide] = final[4 * k:4 * k + 4, :].astype(BF)
+
+    for copy in along_z + to_x + to_y + on_x + on_y:
+        copy.wait_send()
+    for slot in range(4):
+        to_mate(slot, 0).wait_send()
+        to_mate(slot, 1).wait_send()
+    for copy in to_core + first + second + last:
+        copy.wait_send()
+
+
+def store_kernel(*refs):
+    count = len(refs) // 2
+    sources, targets, sems = refs[:count], refs[count:2 * count], refs[-1]
+    copies = [
+        pltpu.make_async_copy(src, dst, sems.at[i])
+        for i, (src, dst) in enumerate(zip(sources, targets))
+    ]
+    for copy in copies:
+        copy.start()
+    for copy in copies:
+        copy.wait()
+
+
+def fused(
+    hidden_in, out_grad, step_ids, segment_ids, advantage_codes, gate_weight, up_weight, down_weight
+):
+    features, units = gate_weight.shape
+    local_tokens = hidden_in.shape[0]
+    tokens = 32 * local_tokens
+    wide = features // 4
+    vmem = pl.BlockSpec(memory_space=pltpu.VMEM)
+    hbm = pl.BlockSpec(memory_space=pl.ANY)
+    dma = pltpu.SemaphoreType.DMA
+    shapes = (
+        jax.ShapeDtypeStruct(hidden_in.shape, BF),
+        jax.ShapeDtypeStruct((units, features), BF),
+        jax.ShapeDtypeStruct((units, features), BF),
+        jax.ShapeDtypeStruct((units, features), BF),
+    )
+    grads = pl.pallas_call(
+        gather_kernel,
+        out_shape=shapes,
+        in_specs=[hbm] * 8,
+        out_specs=(vmem,) * 4,
+        scratch_shapes=[
+            pltpu.VMEM((units, features), BF),
+            pltpu.VMEM((units, features), BF),
+            pltpu.VMEM((units, features), BF),
+            pltpu.VMEM((tokens, features), BF),
+            pltpu.VMEM((local_tokens, features), BF),
+            pltpu.VMEM((local_tokens, features), BF),
+            pltpu.SMEM((local_tokens,), jnp.int32),
+            pltpu.SMEM((local_tokens,), jnp.int32),
+            pltpu.SMEM((local_tokens,), jnp.int32),
+            pltpu.VMEM((8, 4, 16, LANES + 2 * wide), BF),
+            pltpu.VMEM((8, 16, LANES + 2 * features), BF),
+            pltpu.VMEM((4, 4, 16, wide), BF),
+            pltpu.VMEM((4, 4, 16, wide), BF),
+            pltpu.VMEM((4, 4, 16, wide), F32),
+            pltpu.VMEM((4, 2, 16, wide), BF),
+            pltpu.VMEM((4, 2, 16, wide), BF),
+            pltpu.VMEM((4, 2, 16, wide), F32),
+            pltpu.VMEM((4, 16, wide), BF),
+            pltpu.VMEM((4, 16, wide), BF),
+            pltpu.VMEM((4, 16, wide), F32),
+            pltpu.VMEM((16, wide), F32),
+            pltpu.VMEM((3, 16, wide), BF),
+            pltpu.VMEM((3, 16, wide), BF),
+            dma((8,)),
+            dma((3,)), dma((3,)),
+            dma((4,)), dma((4,)), dma((4,)), dma((4,)),
+            dma((4,)), dma((4,)), dma((4,)), dma((4,)),
+            dma((8,)), dma((8,)),
+            dma((4,)), dma((4,)), dma((4,)), dma((4,)), dma((4,)), dma((4,)),
+            dma((3,)), dma((3,)),
+        ],
+        compiler_params=pltpu.CompilerParams(
+            collective_id=0, has_side_effects=True, vmem_limit_bytes=36 * 1024 * 1024
+        ),
+        name="gather_and_sum",
+    )(*[
+        pltpu.with_memory_space_constraint(value, pltpu.HBM)
+        for value in (
+            hidden_in, out_grad, step_ids, segment_ids, advantage_codes,
+            gate_weight.T, up_weight.T, down_weight,
+        )
+    ])
+    input_grad, gate_grad, up_grad, down_grad = pl.pallas_call(
+        store_kernel,
+        out_shape=shapes,
+        in_specs=[hbm] * 4,
+        out_specs=(hbm,) * 4,
+        scratch_shapes=[dma((4,))],
+        name="store",
+    )(*grads)
+    return (input_grad, gate_grad.T, up_grad.T, down_grad)
 
 
 def local(
@@ -75,4 +426,5 @@
         P(("groups", "mp"), "ffn"),
         P(("groups", "ffn"), "mp"),
     )
-    return jax.shard_map(local, mesh=mesh, in_specs=in_specs, out_specs=out_specs, check_vma=False)
+    whole = mesh.shape["groups"] == 1 and mesh.shape["mp"] == 1 and mesh.shape["ffn"] == 32
+    return jax.shard_map(fused if whole else local, mesh=mesh, in_specs=in_specs, out_specs=out_specs, check_vma=False)

time: 204 us -> 213 us (1.044)
  Pallas kernels: 0 us -> 208 us
  blocking collectives: 104 us -> 0 us
  waiting for transfers between devices: 66.7 us -> 0 us
  matrix products: 13.8 us -> 0 us
  between operations: 14.1 us -> 0.65 us
    pallas_call x0 -> x2, Pallas kernels: none -> 208 us  [the longest x1 169 us: fused(): pl.pallas_call(store_kernel, out_shape=shapes, in_specs=[hbm] * 4, out_sp...]
    all_gather x2 -> x0, waiting for transfers between devices: 65.3 us -> none  [the longest x1 51.4 us: local(): lax.all_gather(out_grad, 'ffn', axis=0, tiled=True)]
    unnamed x1 -> x0, blocking collectives: 60.3 us -> none
    all_gather x1 -> x0, blocking collectives: 43.4 us -> none  [local(): lax.all_gather(jnp.stack([step_ids, segment_ids, advantage_codes]), 'ffn'...]
    dot_general x9 -> x0, matrix products: 13.8 us -> none  [the longest x3 5.64 us: contract_first(): lax.dot_general(left, right, (((0,), (0,)), ((), ())), preferred_element_...]
    convert_element_type x2 -> x0, local copies, waits for them, and re-layouts: 3.09 us -> none  [the longest x1 2.45 us: local(): grads_all.astype(jnp.float32)]
    unnamed x9 -> x8, local copies, waits for them, and re-layouts: 1.51 us -> 4.33 us
  transfers between devices with their start and end apart: 2 -> 0, of which waited for: 2 -> 0; matrix products, arithmetic and copies ran while one was open for 3% -> 0% of each run, Pallas kernels for 0% -> 0%
where the time goes in v3:
time: 213 us
  Pallas kernels  208 us (98%)
  local copies, waits for them, and re-layouts  4.33 us (2%)
    pallas_call x1, Pallas kernels, fused(): pl.pallas_call(store_kernel, out_shape=shapes, in_specs=[hbm] * 4, out_sp...  169 us
    pallas_call x1, Pallas kernels, fused(): pl.pallas_call(gather_kernel, out_shape=shapes, in_specs=[hbm] * 8, out_s...  39 us
    unnamed x8, local copies, waits for them, and re-layouts  4.33 us

profile of v3, /device:TPU:0, one launch (start us, length us, event | category | flops | bytes accessed | tf_op | source)
XLA Modules:
  0.0 212.9 jit_solution(11393307203844299685)
XLA Ops:
  0.6 39.0 %gather_and_sum.1 = (bf16[4,4096]{1,0:T(4,128)(2,1)S(1)}, bf16[224,4096]{1,0:T(8,128)(2,1)S(1)}, bf16[224,4096]{1,0:T(8,128)(2,1)S(1)}, bf16[224,4096]{1,0:T(8,128)(2,1)S(1)}) custom-call(bf16[4,4096]{1,0:T(4,128)(2,1)} %x_hbm.1, bf16[4,4096]{1,0:T(4,128)(2,1)} %g_hbm.1, s32[4]{0:T(128)} %step_hbm.1, s32[4]{0:T(128)} %segment_hbm.1, s32[4]{0:T(128)} %code_hbm.1, ...), custom_call_target="tpu_custom_call" | custom-call | tf_op jit(solution)/shard_map/gather_and_sum/pallas_call | solution.py:323
  39.6 0.0 copy-start
  39.6 1.2 copy-done
  40.9 0.0 copy-start.1
  40.9 1.2 copy-done.1
  42.1 0.0 copy-start.2
  42.1 1.2 copy-done.2
  43.4 0.0 copy-start.3
  43.4 0.6 copy-done.3
  44.0 168.9 %store.1 = (bf16[4,4096]{1,0:T(4,128)(2,1)}, bf16[224,4096]{1,0:T(8,128)(2,1)}, bf16[224,4096]{1,0:T(8,128)(2,1)}, bf16[224,4096]{1,0:T(8,128)(2,1)}) custom-call(bf16[4,4096]{1,0:T(4,128)(2,1)} %copy-done.3, bf16[224,4096]{1,0:T(8,128)(2,1)} %copy-done, bf16[224,4096]{1,0:T(8,128)(2,1)} %copy-done.1, bf16[224,4096]{1,0:T(8,128)(2,1)} %copy-done.2), custom_call_target="tpu_custom_call" | custom-call | tf_op jit(solution)/shard_map/store/pallas_call | solution.py:371
Async XLA Ops:
  39.6 1.2 copy-start
  40.9 1.2 copy-start.1
  42.1 1.3 copy-start.2
  43.4 0.6 copy-start.3

commit v4 on v3

--- a/solution.py
+++ b/solution.py
@@ -291,19 +291,6 @@
         copy.wait_send()
 
 
-def store_kernel(*refs):
-    count = len(refs) // 2
-    sources, targets, sems = refs[:count], refs[count:2 * count], refs[-1]
-    copies = [
-        pltpu.make_async_copy(src, dst, sems.at[i])
-        for i, (src, dst) in enumerate(zip(sources, targets))
-    ]
-    for copy in copies:
-        copy.start()
-    for copy in copies:
-        copy.wait()
-
-
 def fused(
     hidden_in, out_grad, step_ids, segment_ids, advantage_codes, gate_weight, up_weight, down_weight
 ):
@@ -320,7 +307,7 @@
         jax.ShapeDtypeStruct((units, features), BF),
         jax.ShapeDtypeStruct((units, features), BF),
     )
-    grads = pl.pallas_call(
+    input_grad, gate_grad, up_grad, down_grad = pl.pallas_call(
         gather_kernel,
         out_shape=shapes,
         in_specs=[hbm] * 8,
@@ -368,14 +355,6 @@
             gate_weight.T, up_weight.T, down_weight,
         )
     ])
-    input_grad, gate_grad, up_grad, down_grad = pl.pallas_call(
-        store_kernel,
-        out_shape=shapes,
-        in_specs=[hbm] * 4,
-        out_specs=(hbm,) * 4,
-        scratch_shapes=[dma((4,))],
-        name="store",
-    )(*grads)
     return (input_grad, gate_grad.T, up_grad.T, down_grad)
 
 

time: 213 us -> 44.1 us (0.21)
  Pallas kernels: 208 us -> 39 us
    pallas_call x1 -> x0, Pallas kernels: 169 us -> none  [fused(): pl.pallas_call(store_kernel, out_shape=shapes, in_specs=[hbm] * 4, out_sp...]
    unnamed x8 -> x4, local copies, waits for them, and re-layouts: 4.33 us -> 4.3 us
where the time goes in v4:
time: 44.1 us; the launch traced here: 43.9 us
  Pallas kernels  39 us (88%)
  local copies, waits for them, and re-layouts  4.3 us (10%)
  between operations  0.64 us (1%)
    pallas_call x1, Pallas kernels, fused(): pl.pallas_call(gather_kernel, out_shape=shapes, in_specs=[hbm] * 8, out_s...  39 us
    unnamed x4, local copies, waits for them, and re-layouts  4.3 us

profile of v4, /device:TPU:0, one launch (start us, length us, event | category | flops | bytes accessed | tf_op | source)
XLA Modules:
  0.0 43.9 jit_solution(18161382948918133726)
XLA Ops:
  0.6 39.0 %gather_and_sum.1 = (bf16[4,4096]{1,0:T(4,128)(2,1)S(1)}, bf16[224,4096]{1,0:T(8,128)(2,1)S(1)}, bf16[224,4096]{1,0:T(8,128)(2,1)S(1)}, bf16[224,4096]{1,0:T(8,128)(2,1)S(1)}) custom-call(bf16[4,4096]{1,0:T(4,128)(2,1)} %x_hbm.1, bf16[4,4096]{1,0:T(4,128)(2,1)} %g_hbm.1, s32[4]{0:T(128)} %step_hbm.1, s32[4]{0:T(128)} %segment_hbm.1, s32[4]{0:T(128)} %code_hbm.1, ...), custom_call_target="tpu_custom_call" | custom-call | tf_op jit(solution)/shard_map/gather_and_sum/pallas_call | solution.py:310
  39.6 0.6 %copy.16 = bf16[4,4096]{1,0:T(4,128)(2,1)} copy(bf16[4,4096]{1,0:T(4,128)(2,1)S(1)} %get-tuple-element.16) | data formatting | bytes 65536
  40.2 1.2 %copy.17 = bf16[4096,224]{0,1:T(8,128)(2,1)} copy(bf16[4096,224]{0,1:T(8,128)(2,1)S(1)} %bitcast.5) | data formatting | bytes 3670016
  41.5 1.2 %copy.18 = bf16[4096,224]{0,1:T(8,128)(2,1)} copy(bf16[4096,224]{0,1:T(8,128)(2,1)S(1)} %bitcast.4) | data formatting | bytes 3670016
  42.7 1.2 %copy.19 = bf16[224,4096]{1,0:T(8,128)(2,1)} copy(bf16[224,4096]{1,0:T(8,128)(2,1)S(1)} %get-tuple-element.19) | data formatting | bytes 3670016

commit v5 on v4

--- a/solution.py
+++ b/solution.py
@@ -42,7 +42,7 @@
     gate_w, up_w, down_w, weighted_all, x_ref, g_ref, step_ref, segment_ref, code_ref,
     raw, rows, core_out, core_in, sums, first_out, first_in,
     halves, second_out, second_in, blocks, last_keep, last_out, last_in,
-    load_sem, za_send, za_recv, x_send, x_recv, y_send, y_recv, fx_send, fx_recv, fy_send, fy_recv,
+    load_sem, za_send, za_recv, x_send, x_recv, y_send, y_recv, d_send, d_recv,
     m_send, m_recv,
     core_send, core_recv, first_send, first_recv, second_send, second_recv, z_send, z_recv,
 ):
@@ -57,6 +57,7 @@
     mate = me + 1 - 2 * core
     xnbr = me + 2 - 4 * x
     ynbr = me + 4 - 8 * y
+    across_xy = xnbr + 4 - 8 * y
     ahead = [me] + [lax.rem(z + d, 4) * 8 + lax.rem(me, 8) for d in (1, 2, 3)]
     behind = [me] + [lax.rem(z + 4 - d, 4) * 8 + lax.rem(me, 8) for d in (1, 2, 3)]
 
@@ -77,7 +78,7 @@
         )
 
     barrier = pltpu.get_barrier_semaphore()
-    for partner in [mate, xnbr, ynbr] + ahead[1:]:
+    for partner in [mate, xnbr, ynbr, across_xy] + ahead[1:]:
         pl.semaphore_signal(barrier, inc=1, device_id={"ffn": partner}, device_id_type=MESH)
 
     for load in loads[:5]:
@@ -96,24 +97,15 @@
     raw[0, 0, :, 0:LANES] = labels.astype(BF)
     raw[0, 0, :, LANES:LANES + wide] = fold(x_ref).astype(BF)
     raw[0, 0, :, LANES + wide:LANES + 2 * wide] = fold(g_ref).astype(BF)
-    pl.semaphore_wait(barrier, 6)
-
-    xp = pl.ds(0, LANES + wide)
-    gp = pl.ds(LANES + wide, wide)
+    pl.semaphore_wait(barrier, 7)
+
     along_z = [
         remote(raw.at[0, 0], raw.at[0, d], za_send.at[d - 1], za_recv.at[d - 1], ahead[d])
         for d in (1, 2, 3)
     ]
     to_x = [remote(raw.at[0, d], raw.at[2, d], x_send.at[d], x_recv.at[d], xnbr) for d in range(4)]
     to_y = [remote(raw.at[0, d], raw.at[1, d], y_send.at[d], y_recv.at[d], ynbr) for d in range(4)]
-    on_x = [
-        remote(raw.at[1, d, :, xp], raw.at[3, d, :, xp], fx_send.at[d], fx_recv.at[d], xnbr)
-        for d in range(4)
-    ]
-    on_y = [
-        remote(raw.at[2, d, :, gp], raw.at[3, d, :, gp], fy_send.at[d], fy_recv.at[d], ynbr)
-        for d in range(4)
-    ]
+    to_d = [remote(raw.at[0, d], raw.at[3, d], d_send.at[d], d_recv.at[d], across_xy) for d in range(4)]
 
     def to_mate(slot, half):
         pieces = pl.ds(2 * half, 2)
@@ -121,12 +113,6 @@
         return remote(
             raw.at[slot, pieces], raw.at[4 + slot, pieces], m_send.at[i], m_recv.at[i], mate
         )
-
-    def onward(d):
-        to_y[d].wait_recv()
-        on_x[d].start()
-        to_x[d].wait_recv()
-        on_y[d].start()
 
     def unfold(slot):
         pieces = [raw[slot, d].astype(F32) for d in range(4)]
@@ -141,35 +127,30 @@
                     [piece[4 * c:4 * c + 4, lo:lo + wide] for piece in pieces], axis=0
                 ).astype(BF)
 
+    def spread(d):
+        to_d[d].start()
+        to_y[d].start()
+        to_x[d].start()
+
+    def arrive(half):
+        for copies, slot in ((to_y, 1), (to_x, 2), (to_d, 3)):
+            for d in (2 * half, 2 * half + 1):
+                copies[d].wait_recv()
+            to_mate(slot, half).start()
+
     for copy in along_z:
         copy.start()
-    to_y[0].start()
-    to_x[0].start()
+    spread(0)
     for d in (1, 2, 3):
         along_z[d - 1].wait_recv()
-        to_y[d].start()
-        to_x[d].start()
+        spread(d)
         if d % 2 == 1:
             to_mate(0, d // 2).start()
-        onward(d - 1)
-        if d == 2:
-            to_mate(1, 0).start()
-            to_mate(2, 0).start()
     unfold(0)
-    onward(3)
-    to_mate(1, 1).start()
-    to_mate(2, 1).start()
-    for d in (0, 1):
-        on_x[d].wait_recv()
-        on_y[d].wait_recv()
-    to_mate(3, 0).start()
-    unfold(1)
-    unfold(2)
-    for d in (2, 3):
-        on_x[d].wait_recv()
-        on_y[d].wait_recv()
-    to_mate(3, 1).start()
-    unfold(3)
+    arrive(0)
+    arrive(1)
+    for slot in (1, 2, 3):
+        unfold(slot)
     for slot in range(4):
         to_mate(slot, 0).wait_recv()
         to_mate(slot, 1).wait_recv()
@@ -282,7 +263,7 @@
     for k in range(4):
         input_grad_ref[:, k * wide:(k + 1) * wide] = final[4 * k:4 * k + 4, :].astype(BF)
 
-    for copy in along_z + to_x + to_y + on_x + on_y:
+    for copy in along_z + to_x + to_y + to_d:
         copy.wait_send()
     for slot in range(4):
         to_mate(slot, 0).wait_send()
@@ -338,8 +319,7 @@
             pltpu.VMEM((3, 16, wide), BF),
             dma((8,)),
             dma((3,)), dma((3,)),
-            dma((4,)), dma((4,)), dma((4,)), dma((4,)),
-            dma((4,)), dma((4,)), dma((4,)), dma((4,)),
+            dma((4,)), dma((4,)), dma((4,)), dma((4,)), dma((4,)), dma((4,)),
             dma((8,)), dma((8,)),
             dma((4,)), dma((4,)), dma((4,)), dma((4,)), dma((4,)), dma((4,)),
             dma((3,)), dma((3,)),

time: 44.1 us -> 41.9 us (0.950)
  Pallas kernels: 39 us -> 36.8 us
    pallas_call x1, Pallas kernels: 39 us -> 36.8 us  [fused(): pl.pallas_call(gather_kernel, out_shape=shapes, in_specs=[hbm] * 8, out_s...]
where the time goes in v5:
time: 41.9 us; the launch traced here: 41.7 us
  Pallas kernels  36.8 us (88%)
  local copies, waits for them, and re-layouts  4.3 us (10%)
  between operations  0.64 us (2%)
    pallas_call x1, Pallas kernels, fused(): pl.pallas_call(gather_kernel, out_shape=shapes, in_specs=[hbm] * 8, out_s...  36.8 us
    unnamed x4, local copies, waits for them, and re-layouts  4.3 us

profile of v5, /device:TPU:0, one launch (start us, length us, event | category | flops | bytes accessed | tf_op | source)
XLA Modules:
  0.0 41.7 jit_solution(14878128763629288591)
XLA Ops:
  0.6 36.8 %gather_and_sum.1 = (bf16[4,4096]{1,0:T(4,128)(2,1)S(1)}, bf16[224,4096]{1,0:T(8,128)(2,1)S(1)}, bf16[224,4096]{1,0:T(8,128)(2,1)S(1)}, bf16[224,4096]{1,0:T(8,128)(2,1)S(1)}) custom-call(bf16[4,4096]{1,0:T(4,128)(2,1)} %x_hbm.1, bf16[4,4096]{1,0:T(4,128)(2,1)} %g_hbm.1, s32[4]{0:T(128)} %step_hbm.1, s32[4]{0:T(128)} %segment_hbm.1, s32[4]{0:T(128)} %code_hbm.1, ...), custom_call_target="tpu_custom_call" | custom-call | tf_op jit(solution)/shard_map/gather_and_sum/pallas_call | solution.py:291
  37.4 0.6 %copy.16 = bf16[4,4096]{1,0:T(4,128)(2,1)} copy(bf16[4,4096]{1,0:T(4,128)(2,1)S(1)} %get-tuple-element.16) | data formatting | bytes 65536
  38.1 1.2 %copy.17 = bf16[4096,224]{0,1:T(8,128)(2,1)} copy(bf16[4096,224]{0,1:T(8,128)(2,1)S(1)} %bitcast.5) | data formatting | bytes 3670016
  39.3 1.2 %copy.18 = bf16[4096,224]{0,1:T(8,128)(2,1)} copy(bf16[4096,224]{0,1:T(8,128)(2,1)S(1)} %bitcast.4) | data formatting | bytes 3670016
  40.5 1.2 %copy.19 = bf16[224,4096]{1,0:T(8,128)(2,1)} copy(bf16[224,4096]{1,0:T(8,128)(2,1)S(1)} %get-tuple-element.19) | data formatting | bytes 3670016
